TPU v7x, 256 devices: a whole 4x4x8 slice. The times are simulated.
256 devices in a mesh: seq: 32 (over z, x_hi, core), resp: 8 (over x_lo, y).
Axes of the slice: x: 4 (x_hi: 2, x_lo: 2; x = x_hi * 2 + x_lo), y: 4, z: 8, core: 2. Of those that a mesh axis runs over, the one named last changes fastest.
Arguments:
- queries: bfloat16 [8, 32, 128, 128], P('resp', 'seq'), may hold values from -6 to 6
- grad_out: bfloat16 [8, 32, 128, 128], P('resp', 'seq'), may hold values from -6 to 6
- outputs: bfloat16 [8, 32, 128, 128], P('resp', 'seq'), may hold values from -6 to 6
- log_sums: float32 [8, 32, 128], P('resp', 'seq'), may hold values from 3 to 5
- prompt_keys: bfloat16 [32768, 8, 128], P('seq'), may hold values from -6 to 6
- prompt_values: bfloat16 [32768, 8, 128], P('seq'), may hold values from -6 to 6
Outputs:
- grad_queries: bfloat16 [8, 32, 128, 128], P('resp', 'seq')
- grad_keys: bfloat16 [32768, 8, 128], P('seq', 'resp')
- grad_values: bfloat16 [32768, 8, 128], P('seq', 'resp')
All inputs are finite; a program needn't handle non-finite values.
Results may differ from a plain program's by a relative error of at most 0.03.
Values may be sent and summed in bfloat16 or wider, within the bound.
A program may use at most 64 MiB of HBM per device.

v0:
```python
import jax
import jax.numpy as jnp
from jax import lax
from jax.sharding import PartitionSpec as P


def grouped_terms(query, grad_rows, delta_rows, sums_rows, group_keys, group_values):
    scale_factor = query.shape[-1] ** (-0.5)
    scores = (
        jnp.einsum("guld,gpd->gulp", query, group_keys, preferred_element_type=jnp.float32)
        * scale_factor
    )
    weights = jnp.exp(scores - sums_rows[..., None])
    grad_probs = jnp.einsum(
        "guld,gpd->gulp", grad_rows, group_values, preferred_element_type=jnp.float32
    )
    grad_scores = (weights * (grad_probs - delta_rows[..., None]) * scale_factor).astype(
        jnp.bfloat16
    )
    grad_query = jnp.einsum(
        "gulp,gpd->guld", grad_scores, group_keys, preferred_element_type=jnp.float32
    )
    grad_key = jnp.einsum("gulp,guld->gpd", grad_scores, query, preferred_element_type=jnp.float32)
    grad_value = jnp.einsum(
        "gulp,guld->gpd",
        weights.astype(jnp.bfloat16),
        grad_rows,
        preferred_element_type=jnp.float32,
    )
    return (grad_query, grad_key, grad_value)


def per_device(queries, grad_out, outputs, log_sums, prompt_keys, prompt_values):
    row_delta = jnp.sum(grad_out.astype(jnp.float32) * outputs.astype(jnp.float32), axis=-1)
    kv_total = prompt_keys.shape[1]
    all_sums, all_delta = (
        lax.all_gather(log_sums, "seq", axis=1, tiled=True),
        lax.all_gather(row_delta, "seq", axis=1, tiled=True),
    )
    heads_total = all_sums.shape[1]
    per_group = heads_total // kv_total
    keys_by_head = jnp.transpose(prompt_keys, (1, 0, 2))
    values_by_head = jnp.transpose(prompt_values, (1, 0, 2))
    zeros_kv = jnp.zeros(keys_by_head.shape, jnp.float32)
    zeros_query = jnp.zeros((1, heads_total) + queries.shape[2:], jnp.float32)
    query_piece = lax.all_gather(queries, "seq", axis=1, tiled=True)
    grad_piece = lax.all_gather(grad_out, "seq", axis=1, tiled=True)
    head_count = query_piece.shape[1]
    sums_piece = all_sums[0]
    delta_piece = all_delta[0]
    head_ids = jnp.arange(head_count, dtype=jnp.int32)

    def one_head(state, inputs):
        grad_query, grad_key, grad_value = state
        query_head, grad_head, sums_head, delta_head, head_id = inputs
        group_id = head_id // per_group
        head_keys = lax.dynamic_index_in_dim(keys_by_head, group_id, 0, keepdims=True)
        head_values = lax.dynamic_index_in_dim(values_by_head, group_id, 0, keepdims=True)
        part_query, part_key, part_value = grouped_terms(
            query_head[None, None],
            grad_head[None, None],
            delta_head[None, None],
            sums_head[None, None],
            head_keys,
            head_values,
        )
        grad_query = lax.dynamic_update_index_in_dim(grad_query, part_query[0, 0][None], head_id, 1)
        old_key = lax.dynamic_index_in_dim(grad_key, group_id, 0, keepdims=True)
        old_value = lax.dynamic_index_in_dim(grad_value, group_id, 0, keepdims=True)
        grad_key = lax.dynamic_update_slice_in_dim(grad_key, old_key + part_key, group_id, 0)
        grad_value = lax.dynamic_update_slice_in_dim(
            grad_value, old_value + part_value, group_id, 0
        )
        return ((grad_query, grad_key, grad_value), None)

    result, unused = lax.scan(
        one_head,
        (zeros_query, zeros_kv, zeros_kv),
        (query_piece[0], grad_piece[0], sums_piece, delta_piece, head_ids),
    )
    grad_query, grad_key, grad_value = result
    own_query = lax.psum_scatter(
        grad_query.astype(jnp.bfloat16), "seq", scatter_dimension=1, tiled=True
    )
    rounded_key = jnp.transpose(grad_key.astype(jnp.bfloat16).astype(jnp.float32), (1, 0, 2))
    rounded_value = jnp.transpose(grad_value.astype(jnp.bfloat16).astype(jnp.float32), (1, 0, 2))
    sum_key, sum_value = (
        lax.psum_scatter(
            rounded_key.astype(jnp.bfloat16), "resp", scatter_dimension=1, tiled=True
        ).astype(jnp.float32),
        lax.psum_scatter(
            rounded_value.astype(jnp.bfloat16), "resp", scatter_dimension=1, tiled=True
        ).astype(jnp.float32),
    )
    return (own_query, sum_key.astype(jnp.bfloat16), sum_value.astype(jnp.bfloat16))


def solution(mesh):
    in_specs = (
        P("resp", "seq", None, None),
        P("resp", "seq", None, None),
        P("resp", "seq", None, None),
        P("resp", "seq", None),
        P("seq", None, None),
        P("seq", None, None),
    )
    out_specs = (P("resp", "seq", None, None), P("seq", "resp", None), P("seq", "resp", None))
    return jax.shard_map(
        per_device, mesh=mesh, in_specs=in_specs, out_specs=out_specs, check_vma=False
    )
```

profile of v0, /device:TPU:16, one launch (start us, length us, event | category | flops | bytes accessed | tf_op | source)
XLA Modules:
  0.0 743.0 jit_solution(1558454881050603627)
XLA Ops:
  9.6 44.5 %all-gather.1 = f32[32,1,128]{2,1,0:T(1,128)S(1)} all-gather(f32[1,1,128]{2,1,0:T(1,128)S(1)} %bitcast.91), channel_id=2, replica_groups=mesh['seq'=32,'resp'=8] {'seq'}, dimensions={0}, use_global_device_ids=true | all-gather | bytes 16896 | tf_op jit(solution)/shard_map/all_gather | solution.py:38
  54.1 36.6 %all_gather.13 = f32[1,32,128]{2,0,1:T(1,128)S(1)} all-gather(f32[1,1,128]{2,0,1:T(1,128)} %bitcast.92), channel_id=1, replica_groups=mesh['seq'=32,'resp'=8] {'seq'}, dimensions={1}, use_global_device_ids=true | all-gather | bytes 16896 | tf_op jit(solution)/shard_map/all_gather | solution.py:37
  90.7 4.3 copy_bitcast_fusion
  95.0 73.3 %all-gather.7.cloned.1.call-done = bf16[1,32,128,128]{3,2,0,1:T(8,128)(2,1)} async-done(((bf16[1,1,128,128]{3,2,0,1:T(8,128)(2,1)}), bf16[1,32,128,128]{3,2,0,1:T(8,128)(2,1)}) %all-gather.7.cloned.1.call-update) | async-done | bytes 1048592 | tf_op jit(solution)/shard_map/all_gather | solution.py:47
  168.6 2.3 broadcast_in_dim.6.clone
  170.9 2.3 broadcast_in_dim.6
  173.2 359.3 %while.16 = (s32[]{:T(128)}, bf16[1,32,128,128]{3,2,1,0:T(8,128)(2,1)S(1)}, f32[8,1024,128]{2,1,0:T(8,128)}, f32[8,1024,128]{2,1,0:T(8,128)}, bf16[32,128,128]{2...) while((s32[]{:T(128)}, ...), condition=%wide.region_2.3_spmd, body=%wide.region_1.2_spmd.sunk | while | flops 168951824 | bytes 5442998 | solution.py:76
  180.2 2.1 fusion.65
  191.4 2.1 fusion.65
  202.6 2.1 fusion.65
  213.8 2.1 fusion.65
  225.1 2.1 fusion.65
  236.3 2.1 fusion.65
  247.5 2.1 fusion.65
  258.7 2.1 fusion.65
  269.9 2.1 fusion.65
  272.1 2.1 fusion.64
  281.2 2.1 fusion.65
  283.3 2.1 fusion.64
  292.4 2.1 fusion.65
  294.6 2.1 fusion.64
  303.7 2.1 fusion.65
  305.8 2.1 fusion.64
  359.8 2.1 fusion.65
  362.0 2.1 fusion.64
  371.1 2.1 fusion.65
  373.2 2.1 fusion.64
  382.3 2.1 fusion.65
  384.5 2.1 fusion.64
  393.6 2.1 fusion.65
  395.7 2.1 fusion.64
  404.8 2.1 fusion.65
  406.9 2.1 fusion.64
  416.0 2.1 fusion.65
  418.2 2.1 fusion.64
  427.3 2.1 fusion.65
  429.4 2.1 fusion.64
  438.5 2.1 fusion.65
  440.6 2.1 fusion.64
  494.5 2.2 fusion.65
  505.8 2.2 fusion.65
  517.0 2.2 fusion.65
  528.3 2.2 fusion.65
  533.6 3.9 convert_bitcast_fusion
  537.6 3.9 convert_bitcast_fusion.1
  541.4 104.4 %reduce-scatter.4.cloned.1.call-done = bf16[1,1,128,128]{3,2,1,0:T(8,128)(2,1)} async-done(((bf16[1,32,128,128]{3,2,1,0:T(8,128)(2,1)}), bf16[1,1,128,128]{3,2,1,0:T(8,128)(2,1)}) %reduce-scatter.4.cloned.1.call-update) | async-done | bytes 32784 | tf_op jit(solution)/shard_map/reduce_scatter | solution.py:82
  645.9 44.1 %reduce-scatter.8.cloned.1.call-done = bf16[1024,1,128]{2,0,1:T(8,128)(2,1)} async-done(((bf16[1024,8,128]{2,0,1:T(8,128)(2,1)}), bf16[1024,1,128]{2,0,1:T(8,128)(2,1)}) %reduce-scatter.8.cloned.1.call-update) | async-done | bytes 262160 | tf_op jit(solution)/shard_map/reduce_scatter | solution.py:91
  690.0 46.5 %reduce-scatter.6.cloned.1.call-done = bf16[1024,1,128]{2,0,1:T(8,128)(2,1)} async-done(((bf16[1024,8,128]{2,0,1:T(8,128)(2,1)}), bf16[1024,1,128]{2,0,1:T(8,128)(2,1)}) %reduce-scatter.6.cloned.1.call-update) | async-done | bytes 262160 | tf_op jit(solution)/shard_map/reduce_scatter | solution.py:88
  (204 shorter events, 160.5 us)
Async XLA Ops:
  7.2 87.9 %all-gather.5.cloned.1.call-start = ((), (), s32[]{:S(2)}) async-start(), calls=%async_computation.3 | async-start | bytes 1081344 | tf_op jit(solution)/shard_map/all_gather | solution.py:46
  7.9 160.5 %all-gather.7.cloned.1.call-start = ((), (), s32[]{:S(2)}) async-start(), calls=%async_computation.4 | async-start | bytes 1081344 | tf_op jit(solution)/shard_map/all_gather | solution.py:47
  8.6 637.2 %reduce-scatter.4.cloned.1.call-start = ((), (), s32[]{:S(2)}) async-start(), calls=%async_computation.5 | async-start | bytes 1081344 | tf_op jit(solution)/shard_map/reduce_scatter | solution.py:82
  532.5 1.0 copy-start
  533.6 156.4 %reduce-scatter.8.cloned.1.call-start = ((), (), s32[]{:S(2)}) async-start(), calls=%async_computation.7 | async-start | bytes 2359296 | tf_op jit(solution)/shard_map/reduce_scatter | solution.py:91
  537.5 199.0 %reduce-scatter.6.cloned.1.call-start = ((), (), s32[]{:S(2)}) async-start(), calls=%async_computation.6 | async-start | bytes 2359296 | tf_op jit(solution)/shard_map/reduce_scatter | solution.py:88
Sparse Core Ops, SparseCore 0:
  10.8 80.2 all-gather.4
  93.9 74.3 all-gather.6
  533.7 112.1 reduce-scatter.3
  649.0 40.9 reduce-scatter.7
  693.1 43.3 reduce-scatter.5
where the time goes:
time: 752 us; the launch traced here: 743 us
  waiting for transfers between devices  270 us (36%)
  matrix products  215 us (29%)
  loops' own time  126 us (17%)
  blocking collectives  81.1 us (11%)
  local copies, waits for them, and re-layouts  29.2 us (4%)
  between operations  13.8 us (2%)
  other arithmetic  8.61 us (1%)
    another operation x1, loops' own time, per_device(): lax.scan(one_head, (zeros_query, zeros_kv, zeros_kv), (query_piece[0], gr...  126 us
    reduce_scatter x1, waiting for transfers between devices, per_device(): lax.psum_scatter(grad_query.astype(jnp.bfloat16), 'seq', scatter_dimensio...  104 us
    all_gather x1, waiting for transfers between devices, per_device(): grad_piece = lax.all_gather(grad_out, 'seq', axis=1, tiled=True)  73.3 us
    dot_general x32, matrix products, grouped_terms(): jnp.einsum('gulp,guld->gpd', weights.astype(jnp.bfloat16), grad_rows, pre...  68.2 us
    dot_general x32, matrix products, grouped_terms(): jnp.einsum('gulp,guld->gpd', grad_scores, query, preferred_element_type=j...  67.7 us
    reduce_scatter x1, waiting for transfers between devices, per_device(): lax.psum_scatter(rounded_key.astype(jnp.bfloat16), 'resp', scatter_dimens...  46.5 us
    all_gather x1, blocking collectives, per_device(): lax.all_gather(row_delta, 'seq', axis=1, tiled=True)  44.5 us
    reduce_scatter x1, waiting for transfers between devices, per_device(): lax.psum_scatter(rounded_value.astype(jnp.bfloat16), 'resp', scatter_dime...  44.1 us
  transfers between devices with their start and end apart: 5, of which 4 were waited for; matrix products, arithmetic and copies ran while one was open for 2% of the time, Pallas kernels for 0%

commit v1 on v0

v1 whole, which is shorter than its diff:
```python
import jax
import jax.numpy as jnp
from jax import lax
from jax.experimental import pallas as pl
from jax.experimental.pallas import tpu as pltpu
from jax.sharding import PartitionSpec as P

NT = (((1,), (1,)), ((), ()))
NN = (((1,), (0,)), ((), ()))
LOG2E = 1.4426950408889634
CHUNK = 4
STEP = 512


def group_kernel(rows_ref, stats_ref, keys_ref, values_ref, dq_ref, dk_ref, dv_ref, keys_t, acc_k, acc_v):
    blocks, _, rows, dim = rows_ref.shape
    positions = keys_ref.shape[0]
    scale = dim**-0.5
    keys_t[...] = keys_ref[...].T
    acc_k[...] = jnp.zeros_like(acc_k)
    acc_v[...] = jnp.zeros_like(acc_v)

    @pl.loop(0, blocks // CHUNK)
    def _(step):
        first = step * CHUNK
        query = jnp.concatenate([rows_ref[first + j, 0] for j in range(CHUNK)], axis=0)
        grad = jnp.concatenate([rows_ref[first + j, 1] for j in range(CHUNK)], axis=0)
        sums = jnp.concatenate([stats_ref[first + j, 0:1, :] for j in range(CHUNK)], axis=1) * LOG2E
        delta = jnp.concatenate([stats_ref[first + j, 1:2, :] for j in range(CHUNK)], axis=1)
        total = None
        for at in range(0, positions, STEP):
            part = pl.ds(at, STEP)
            keys = keys_ref[part, :]
            scores = lax.dot_general(keys, query, NT, preferred_element_type=jnp.float32)
            probs = lax.dot_general(values_ref[part, :], grad, NT, preferred_element_type=jnp.float32)
            weights = jnp.exp2(scores * (scale * LOG2E) - sums)
            low = weights.astype(jnp.bfloat16)
            grad_scores = (weights * (probs - delta)).astype(jnp.bfloat16)
            acc_v[part, :] += lax.dot_general(low, grad, NN, preferred_element_type=jnp.float32)
            acc_k[part, :] += lax.dot_general(grad_scores, query, NN, preferred_element_type=jnp.float32)
            term = lax.dot_general(keys_t[:, part], grad_scores, NN, preferred_element_type=jnp.float32)
            total = term if total is None else total + term
        total = (total * scale).astype(jnp.bfloat16)
        for j in range(CHUNK):
            dq_ref[first + j] = total[:, j * rows : (j + 1) * rows]

    dk_ref[...] = (acc_k[...] * scale).astype(dk_ref.dtype)
    dv_ref[...] = acc_v[...].astype(dv_ref.dtype)


def grouped(rows, stats, keys, values):
    vmem = pl.BlockSpec(memory_space=pltpu.VMEM)
    blocks, _, length, dim = rows.shape
    positions = keys.shape[0]
    return pl.pallas_call(
        group_kernel,
        out_shape=(
            jax.ShapeDtypeStruct((blocks, dim, length), jnp.bfloat16),
            jax.ShapeDtypeStruct((positions, dim), jnp.bfloat16),
            jax.ShapeDtypeStruct((positions, dim), jnp.bfloat16),
        ),
        in_specs=[vmem] * 4,
        out_specs=(vmem,) * 3,
        scratch_shapes=[
            pltpu.VMEM((dim, positions), jnp.bfloat16),
            pltpu.VMEM((positions, dim), jnp.float32),
            pltpu.VMEM((positions, dim), jnp.float32),
        ],
        compiler_params=pltpu.CompilerParams(vmem_limit_bytes=40 << 20),
    )(rows, stats, keys, values)


def per_device(queries, grad_out, outputs, log_sums, prompt_keys, prompt_values):
    both = ("seq", "resp")
    there = [
        ((4 * g + j) * 8 + r, (4 * r + j) * 8 + g) for g in range(8) for j in range(4) for r in range(8)
    ]
    back = [(b, a) for a, b in there]
    group = lax.axis_index("resp")
    delta = jnp.sum(grad_out.astype(jnp.float32) * outputs.astype(jnp.float32), axis=-1)
    stats = jnp.stack([log_sums[0, 0], delta[0, 0]])
    rows = jnp.stack([queries[0, 0], grad_out[0, 0]])
    rows = lax.all_gather(lax.ppermute(rows, both, there), "seq", axis=0, tiled=False)
    stats = lax.all_gather(lax.ppermute(stats, both, there), "seq", axis=0, tiled=False)
    keys = lax.dynamic_index_in_dim(prompt_keys, group, 1, keepdims=False)
    values = lax.dynamic_index_in_dim(prompt_values, group, 1, keepdims=False)
    dq, dk, dv = grouped(rows, stats, keys, values)
    own = lax.psum_scatter(dq, "seq", scatter_dimension=0, tiled=True)
    own = lax.ppermute(own, both, back)
    return jnp.swapaxes(own, 1, 2)[None], dk[:, None, :], dv[:, None, :]


def solution(mesh):
    in_specs = (
        P("resp", "seq", None, None),
        P("resp", "seq", None, None),
        P("resp", "seq", None, None),
        P("resp", "seq", None),
        P("seq", None, None),
        P("seq", None, None),
    )
    out_specs = (P("resp", "seq", None, None), P("seq", "resp", None), P("seq", "resp", None))
    return jax.shard_map(
        per_device, mesh=mesh, in_specs=in_specs, out_specs=out_specs, check_vma=False
    )
```

time: 752 us -> 251 us (0.33)
  matrix products: 215 us -> 0 us
  loops' own time: 126 us -> 0 us
  waiting for transfers between devices: 270 us -> 152 us
  blocking collectives: 81.1 us -> 47.8 us
  local copies, waits for them, and re-layouts: 29.2 us -> 6.32 us
  starting transfers between devices: 0.2 us -> 13.9 us
  Pallas kernels: 0 us -> 12.8 us
    dot_general x160 -> x0, matrix products: 215 us -> none  [the longest x32 68.2 us: grouped_terms(): jnp.einsum('gulp,guld->gpd', weights.astype(jnp.bfloat16), grad_rows, pre...]
    another operation x1 -> x0, loops' own time: 126 us -> none  [per_device(): lax.scan(one_head, (zeros_query, zeros_kv, zeros_kv), (query_piece[0], gr...]
    reduce_scatter x3 -> x1, waiting for transfers between devices: 195 us -> 112 us  [per_device(): own = lax.psum_scatter(dq, 'seq', scatter_dimension=0, tiled=True)]
    all_gather x2 -> x1, waiting for transfers between devices: 73.3 us -> 28.4 us  [per_device(): lax.all_gather(lax.ppermute(rows, both, there), 'seq', axis=0, tiled=False)]
    all_gather x2 -> x1, blocking collectives: 81.1 us -> 47.8 us  [per_device(): lax.all_gather(lax.ppermute(stats, both, there), 'seq', axis=0, tiled=False)]
    dynamic_slice x32 -> x1, local copies, waits for them, and re-layouts: 18.6 us -> 3.31 us  [per_device(): values = lax.dynamic_index_in_dim(prompt_values, group, 1, keepdims=False)]
    ppermute x0 -> x3, starting transfers between devices: none -> 13.9 us  [the longest x1 4.94 us: per_device(): lax.ppermute(rows, both, there)]
    pallas_call x0 -> x1, Pallas kernels: none -> 12.8 us  [grouped(): pl.pallas_call(group_kernel, out_shape=(jax.ShapeDtypeStruct((blocks, dim...]
  transfers between devices with their start and end apart: 5 -> 5, of which waited for: 4 -> 5; matrix products, arithmetic and copies ran while one was open for 2% -> 2% of each run, Pallas kernels for 0% -> 0%
where the time goes in v1:
time: 251 us; the launch traced here: 249 us
  waiting for transfers between devices  152 us (61%)
  blocking collectives  47.8 us (19%)
  between operations  14.1 us (6%)
  starting transfers between devices  13.9 us (6%)
  Pallas kernels  12.8 us (5%)
  local copies, waits for them, and re-layouts  6.32 us (3%)
    reduce_scatter x1, waiting for transfers between devices, per_device(): own = lax.psum_scatter(dq, 'seq', scatter_dimension=0, tiled=True)  112 us
    all_gather x1, blocking collectives, per_device(): lax.all_gather(lax.ppermute(stats, both, there), 'seq', axis=0, tiled=False)  47.8 us
    all_gather x1, waiting for transfers between devices, per_device(): lax.all_gather(lax.ppermute(rows, both, there), 'seq', axis=0, tiled=False)  28.4 us
    pallas_call x1, Pallas kernels, grouped(): pl.pallas_call(group_kernel, out_shape=(jax.ShapeDtypeStruct((blocks, dim...  12.8 us
    ppermute x1, waiting for transfers between devices, per_device(): lax.ppermute(rows, both, there)  5.49 us
    ppermute x1, waiting for transfers between devices, per_device(): own = lax.ppermute(own, both, back)  5.26 us
  transfers between devices with their start and end apart: 5, of which 5 were waited for; matrix products, arithmetic and copies ran while one was open for 2% of the time, Pallas kernels for 0%

profile of v1, /device:TPU:16, one launch (start us, length us, event | category | flops | bytes accessed | tf_op | source)
XLA Modules:
  0.0 249.0 jit_solution(17550730487869295262)
XLA Ops:
  7.2 0.0 all-gather.5.cloned.1.call-start
  7.2 0.8 pad_maximum_fusion
  8.0 4.9 %collective-permute-start = (bf16[2,128,128]{2,1,0:T(8,128)(2,1)S(1)}, bf16[2,128,128]{2,1,0:T(8,128)(2,1)S(1)}, u32[]{:S(2)}, u32[]{:S(2)}) collective-permute-start(bf16[2,128,128]{2,1,0:T(8,128)(2,1)S(1)} %pad_maximum_fusion), channel_id=1, source_target_pairs={{0,0},{1,32},{2,64},{3,96},{4,128},{5,160},{6,192},{7,224},{8,8},{... | collective-permute-start | bytes 196616 | tf_op jit(solution)/shard_map/ppermute | solution.py:83
  12.9 5.5 %collective-permute-done = bf16[2,128,128]{2,1,0:T(8,128)(2,1)S(1)} collective-permute-done((bf16[2,128,128]{2,1,0:T(8,128)(2,1)S(1)}, bf16[2,128,128]{2,1,0:T(8,128)(2,1)S(1)}, u32[]{:S(2)}, u32[]{:S(2)}) %collective-permute-start) | collective-permute-done | bytes 65568 | tf_op jit(solution)/shard_map/ppermute | solution.py:83
  18.4 0.0 copy-start.1
  18.4 0.6 copy-done.1
  19.1 0.0 all-gather.5.cloned.1.call-update
  19.1 0.0 reduce-scatter.2.cloned.1.call-start
  19.1 0.9 multiply_reduce_fusion
  20.0 0.7 pad_maximum_fusion.1
  20.7 4.9 %collective-permute-start.1 = (f32[2,128]{1,0:T(2,128)S(1)}, f32[2,128]{1,0:T(2,128)S(1)}, u32[]{:S(2)}, u32[]{:S(2)}) collective-permute-start(f32[2,128]{1,0:T(2,128)S(1)} %pad_maximum_fusion.1), channel_id=1, source_target_pairs={{0,0},{1,32},{2,64},{3,96},{4,128},{5,160},{6,192},{7,224},{8,8},{... | collective-permute-start | bytes 3080 | tf_op jit(solution)/shard_map/ppermute | solution.py:84
  25.6 3.3 %constant_dynamic-slice_fusion = (bf16[1024,1,128]{2,1,0:T(2,128)(2,1)S(1)}, bf16[1024,1,128]{2,1,0:T(2,128)(2,1)S(1)}) fusion(bf16[1024,8,128]{2,1,0:T(8,128)(2,1)} %param.11, s32[]{:T(128)S(6)} %select_n.5, bf16[1024,8,128]{2,1,0:T(8,128)(2,1)} %param.10), kind=kLoop, calls=%fused_computation.5 | loop fusion | bytes 1048580 | tf_op jit(solution)/shard_map/jit(dynamic_index_in_dim)/dynamic_slice | solution.py:86
  29.0 0.5 collective-permute-done.1
  29.4 47.8 %all-gather.2.stats_ref = f32[32,2,128]{2,1,0:T(2,128)S(1)} all-gather(f32[1,2,128]{2,1,0:T(2,128)S(1)} %bitcast.24), channel_id=3, replica_groups=mesh['seq'=32,'resp'=8] {'seq'}, dimensions={0}, use_global_device_ids=true | all-gather | bytes 33792 | tf_op jit(solution)/shard_map/all_gather | solution.py:84
  77.2 28.4 %all-gather.5.cloned.1.call-done = bf16[64,128,128]{2,1,0:T(8,128)(2,1)} async-done(((bf16[2,128,128]{2,1,0:T(8,128)(2,1)}), bf16[64,128,128]{2,1,0:T(8,128)(2,1)}) %all-gather.5.cloned.1.call-update) | async-done | bytes 2097168 | tf_op jit(solution)/shard_map/all_gather | solution.py:83
  105.6 0.0 copy-start
  105.6 1.6 copy-done
  107.2 12.8 %shard_map.85 = (bf16[32,128,128]{2,1,0:T(8,128)(2,1)}, bf16[1024,128]{1,0:T(8,128)(2,1)}, bf16[1024,128]{1,0:T(8,128)(2,1)}) custom-call(bf16[32,2,128,128]{3,2,1,0:T(8,128)(2,1)S(1)} %bitcast.17, f32[32,2,128]{2,1,0:T(2,128)S(1)} %all-gather.2.stats_ref, bf16[1024,128]{1,0:T(8,128)(2,1)S(1)} %bitcast.19, bf16[1024,128]{1,0:T(8,128)(2,1)S(1)} %bitcast.18), custom_call_target="tpu_custom_call" | custom-call | tf_op jit(solution)/shard_map/pallas_call | solution.py:55
  120.0 0.0 reduce-scatter.2.cloned.1.call-update
  120.0 112.1 %reduce-scatter.2.cloned.1.call-done = bf16[1,128,128]{2,1,0:T(8,128)(2,1)} async-done(((bf16[32,128,128]{2,1,0:T(8,128)(2,1)}), bf16[1,128,128]{2,1,0:T(8,128)(2,1)}) %reduce-scatter.2.cloned.1.call-update) | async-done | bytes 32784 | tf_op jit(solution)/shard_map/reduce_scatter | solution.py:88
  232.1 4.0 %collective-permute-start.2 = (bf16[1,128,128]{2,1,0:T(8,128)(2,1)}, bf16[1,128,128]{2,1,0:T(8,128)(2,1)S(1)}, u32[]{:S(2)}, u32[]{:S(2)}) collective-permute-start(bf16[1,128,128]{2,1,0:T(8,128)(2,1)} %reduce-scatter.2.cloned.1.call-done), channel_id=1, source_target_pairs={{0,0},{32,1},{64,2},{96,3},{128,4},{160,5},{192,6},{224,7},{8,8},{... | collective-permute-start | bytes 98312 | tf_op jit(solution)/shard_map/ppermute | solution.py:89
  236.2 5.3 %collective-permute-done.2 = bf16[1,128,128]{2,1,0:T(8,128)(2,1)S(1)} collective-permute-done((bf16[1,128,128]{2,1,0:T(8,128)(2,1)}, bf16[1,128,128]{2,1,0:T(8,128)(2,1)S(1)}, u32[]{:S(2)}, u32[]{:S(2)}) %collective-permute-start.2) | collective-permute-done | bytes 32800 | tf_op jit(solution)/shard_map/ppermute | solution.py:89
  241.4 0.7 copy.15
  (2 shorter events, 0.1 us)
Async XLA Ops:
  7.2 98.4 %all-gather.5.cloned.1.call-start = ((), (), s32[]{:S(2)}) async-start(), calls=%async_computation.2 | async-start | bytes 2162688 | tf_op jit(solution)/shard_map/all_gather | solution.py:83
  8.0 10.4 %collective-permute-start = (bf16[2,128,128]{2,1,0:T(8,128)(2,1)S(1)}, bf16[2,128,128]{2,1,0:T(8,128)(2,1)S(1)}, u32[]{:S(2)}, u32[]{:S(2)}) collective-permute-start(bf16[2,128,128]{2,1,0:T(8,128)(2,1)S(1)} %pad_maximum_fusion), channel_id=1, source_target_pairs={{0,0},{1,32},{2,64},{3,96},{4,128},{5,160},{6,192},{7,224},{8,8},{... | collective-permute-start | bytes 196616 | tf_op jit(solution)/shard_map/ppermute | solution.py:83
  18.4 0.6 copy-start.1
  19.1 213.0 %reduce-scatter.2.cloned.1.call-start = ((), (), s32[]{:S(2)}) async-start(), calls=%async_computation.1 | async-start | bytes 1081344 | tf_op jit(solution)/shard_map/reduce_scatter | solution.py:88
  20.7 8.8 %collective-permute-start.1 = (f32[2,128]{1,0:T(2,128)S(1)}, f32[2,128]{1,0:T(2,128)S(1)}, u32[]{:S(2)}, u32[]{:S(2)}) collective-permute-start(f32[2,128]{1,0:T(2,128)S(1)} %pad_maximum_fusion.1), channel_id=1, source_target_pairs={{0,0},{1,32},{2,64},{3,96},{4,128},{5,160},{6,192},{7,224},{8,8},{... | collective-permute-start | bytes 3080 | tf_op jit(solution)/shard_map/ppermute | solution.py:84
  105.6 1.6 copy-start
  232.1 9.3 %collective-permute-start.2 = (bf16[1,128,128]{2,1,0:T(8,128)(2,1)}, bf16[1,128,128]{2,1,0:T(8,128)(2,1)S(1)}, u32[]{:S(2)}, u32[]{:S(2)}) collective-permute-start(bf16[1,128,128]{2,1,0:T(8,128)(2,1)} %reduce-scatter.2.cloned.1.call-done), channel_id=1, source_target_pairs={{0,0},{32,1},{64,2},{96,3},{128,4},{160,5},{192,6},{224,7},{8,8},{... | collective-permute-start | bytes 98312 | tf_op jit(solution)/shard_map/ppermute | solution.py:89
Sparse Core Ops, SparseCore 0:
  19.2 86.3 all-gather.4
  120.1 111.9 reduce-scatter.1

commit v2 on v1

v2 whole, which is shorter than its diff:
```python
import functools

import jax
import jax.numpy as jnp
from jax import lax
from jax.experimental import pallas as pl
from jax.experimental.pallas import tpu as pltpu
from jax.sharding import PartitionSpec as P

NT = (((1,), (1,)), ((), ()))
NN = (((1,), (0,)), ((), ()))
MESH = pl.DeviceIdType.MESH
LOG2E = 1.4426950408889634
STEP = 512
PLANES = 8
OFFSETS = (0, 7, 1, 6, 2, 5, 3, 4)


def split3(row):
    high = row.astype(jnp.bfloat16).astype(jnp.float32)
    rest = row - high
    mid = rest.astype(jnp.bfloat16).astype(jnp.float32)
    return [high, mid, rest - mid]


def kernel(
    q_ref, g_ref, o_ref, sums_ref, k_hbm, v_hbm,
    dq_ref, dk_ref, dv_ref,
    pack, blk, part, in1, mid, in2, k_all, v_all, keys, values, keys_t, acc_k, acc_v,
    kv_sem, pre_send, pre_recv, up_send, down_send, ring_recv, sib_send, sib_recv,
    one_send, one_recv, two_send, two_recv,
):
    seq, grp = lax.axis_index("seq"), lax.axis_index("resp")
    z, j = seq // 4, lax.rem(seq, 4)
    xh, core = j // 2, lax.rem(j, 2)
    rows = q_ref.shape[0]
    positions = dk_ref.shape[0]
    groups = k_all.shape[0] // positions
    scale = q_ref.shape[1] ** -0.5

    def wrap(value):
        return lax.rem(value + 2 * PLANES, PLANES)

    def remote(src, dst, send, recv, seq_to, resp_to):
        return pltpu.make_async_remote_copy(
            src_ref=src, dst_ref=dst, send_sem=send, recv_sem=recv,
            device_id=(seq_to, resp_to), device_id_type=MESH,
        )

    def arrived(ref, sem):
        pltpu.make_async_copy(ref, ref, sem).wait()

    load_k = pltpu.make_async_copy(k_hbm, k_all, kv_sem.at[0])
    load_v = pltpu.make_async_copy(v_hbm, v_all, kv_sem.at[1])
    load_k.start()
    load_v.start()

    barrier = pltpu.get_barrier_semaphore()
    source = wrap(z - grp)
    pre_seq = wrap(grp + z) * 4 + core
    on_self = jnp.logical_and(grp == 0, z == 0)

    @pl.loop(1, 4 * PLANES)
    def _(t):
        other = lax.rem(grp * 4 + j + t, 4 * PLANES)
        pl.semaphore_signal(
            barrier, inc=1, device_id=(z * 4 + lax.rem(other, 4), other // 4), device_id_type=MESH
        )

    @pl.loop(1, PLANES)
    def _(t):
        pl.semaphore_signal(
            barrier, inc=1, device_id=(lax.rem(z + t, PLANES) * 4 + j, grp), device_id_type=MESH
        )

    for side in range(2):
        here = jnp.logical_and(on_self, xh == side)

        @pl.when(jnp.logical_not(here))
        def _():
            pl.semaphore_signal(
                barrier, inc=1, device_id=(grp * 4 + 2 * side + core, source), device_id_type=MESH
            )

    grad_own = g_ref[...]
    product = grad_own.astype(jnp.float32) * o_ref[...].astype(jnp.float32)
    delta = jnp.sum(product.T, axis=0, keepdims=True)
    stats = split3(sums_ref[...] * LOG2E) + split3(delta)
    stats = jnp.concatenate(stats + [jnp.zeros((10, rows), jnp.float32)], axis=0)
    pack[0:rows, :] = q_ref[...]
    pack[rows : 2 * rows, :] = grad_own
    pack[2 * rows :, :] = stats.astype(jnp.bfloat16)

    pl.semaphore_wait(barrier, 4 * PLANES - 1 + PLANES - 1 + 2 - on_self.astype(jnp.int32))

    def first(side):
        return remote(
            pack, blk.at[0, core, xh], pre_send.at[side], pre_recv.at[xh], pre_seq + 2 * side, z
        )

    for side in range(2):
        here = jnp.logical_and(on_self, xh == side)

        @pl.when(here)
        def _():
            pltpu.make_async_copy(pack, blk.at[0, core, xh], pre_recv.at[xh]).start()

        @pl.when(jnp.logical_not(here))
        def _():
            first(side).start()

    load_k.wait()
    load_v.wait()
    tile = 128
    pick = (
        lax.broadcasted_iota(jnp.int32, (tile, tile * groups), 1)
        == lax.broadcasted_iota(jnp.int32, (tile, tile * groups), 0) * groups + grp
    ).astype(jnp.bfloat16)
    for t in range(positions // tile):
        wide, narrow = pl.ds(t * tile * groups, tile * groups), pl.ds(t * tile, tile)
        keys[narrow, :] = lax.dot_general(
            pick, k_all[wide, :], NN, preferred_element_type=jnp.float32
        ).astype(jnp.bfloat16)
        values[narrow, :] = lax.dot_general(
            pick, v_all[wide, :], NN, preferred_element_type=jnp.float32
        ).astype(jnp.bfloat16)
    keys_t[...] = keys[...].T
    acc_k[...] = jnp.zeros_like(acc_k)
    acc_v[...] = jnp.zeros_like(acc_v)

    above, below = wrap(z + 1) * 4 + j, wrap(z - 1) * 4 + j
    sibling = z * 4 + 2 * xh + (1 - core)

    def to_sibling(k, s):
        return remote(
            blk.at[k, core, s], blk.at[k, core, s], sib_send.at[k, s], sib_recv.at[k, s], sibling, grp
        )

    def onward(k, s):
        copies = []
        if k == 0:
            steps = ((1, 0), (2, 1))
        elif k in (1, 3):
            steps = ((k + 2, 0),)
        elif k in (2, 4):
            steps = ((k + 2, 1),)
        elif k == 5 and s == 0:
            steps = ((7, 0),)
        elif k == 6 and s == 1:
            steps = ((7, 1),)
        else:
            steps = ()
        for k_to, way in steps:
            copies.append(
                remote(
                    blk.at[k, core, s], blk.at[k_to, core, s],
                    (down_send if way else up_send).at[k, s], ring_recv.at[k_to, s],
                    below if way else above, grp,
                )
            )
        return copies

    def pass_on(k):
        for s in range(2):
            arrived(blk.at[k, core, s], (pre_recv.at[s] if k == 0 else ring_recv.at[k, s]))
            for copy in onward(k, s):
                copy.start()
            to_sibling(k, s).start()

    def work(k):
        parts = [blk.at[k, b // 2, b % 2] for b in range(4)]
        query = jnp.concatenate([p[0:rows, :] for p in parts], axis=0)
        grad = jnp.concatenate([p[rows : 2 * rows, :] for p in parts], axis=0)
        stats = [p[2 * rows :, :].astype(jnp.float32) for p in parts]
        sums = jnp.concatenate([s[0:1] + s[1:2] + s[2:3] for s in stats], axis=1)
        delta = jnp.concatenate([s[3:4] + s[4:5] + s[5:6] for s in stats], axis=1)
        total = None
        for at in range(0, positions, STEP):
            span = pl.ds(at, STEP)
            scores = lax.dot_general(keys[span, :], query, NT, preferred_element_type=jnp.float32)
            probs = lax.dot_general(values[span, :], grad, NT, preferred_element_type=jnp.float32)
            weights = jnp.exp2(scores * (scale * LOG2E) - sums)
            low = weights.astype(jnp.bfloat16)
            grad_scores = (weights * (probs - delta)).astype(jnp.bfloat16)
            acc_v[span, :] += lax.dot_general(low, grad, NN, preferred_element_type=jnp.float32)
            acc_k[span, :] += lax.dot_general(grad_scores, query, NN, preferred_element_type=jnp.float32)
            term = lax.dot_general(keys_t[:, span], grad_scores, NN, preferred_element_type=jnp.float32)
            total = term if total is None else total + term
        total = total.astype(jnp.bfloat16)
        for b in range(4):
            part[k, b] = total[:, b * rows : (b + 1) * rows]

    def spread(k, b):
        owner = (b % 2) * 2 + b // 2
        resp_to = wrap(z + OFFSETS[k] - grp)
        here = jnp.logical_and(owner == j, resp_to == grp)
        copy = remote(
            part.at[k, b], in1.at[k, j], one_send.at[k, b], one_recv.at[k, j], z * 4 + owner, resp_to
        )
        return here, copy

    def send_parts(k):
        for b in range(4):
            here, copy = spread(k, b)

            @pl.when(here)
            def _():
                pltpu.make_async_copy(part.at[k, b], in1.at[k, j], one_recv.at[k, j]).start()

            @pl.when(jnp.logical_not(here))
            def _():
                copy.start()

    def home(k):
        plane = wrap(z + OFFSETS[k] - grp)
        copy = remote(mid.at[k], in2.at[k], two_send.at[k], two_recv.at[k], plane * 4 + j, grp)
        return plane == z, copy

    def combine(k):
        for s in range(4):
            arrived(in1.at[k, s], one_recv.at[k, s])
        total = in1[k, 0].astype(jnp.float32)
        for s in range(1, 4):
            total += in1[k, s].astype(jnp.float32)
        mid[k] = total.astype(jnp.bfloat16)
        here, copy = home(k)

        @pl.when(here)
        def _():
            pltpu.make_async_copy(mid.at[k], in2.at[k], two_recv.at[k]).start()

        @pl.when(jnp.logical_not(here))
        def _():
            copy.start()

    for k in range(PLANES):
        if k in (0, 7):
            pass_on(k)
        elif k % 2 == 1:
            pass_on(k)
            pass_on(k + 1)
        for s in range(2):
            arrived(blk.at[k, 1 - core, s], sib_recv.at[k, s])
        work(k)
        send_parts(k)
        if k >= 2:
            combine(k - 2)
    dk_ref[...] = (acc_k[...] * scale).astype(dk_ref.dtype)
    dv_ref[...] = acc_v[...].astype(dv_ref.dtype)
    combine(PLANES - 2)
    combine(PLANES - 1)

    for k in range(PLANES):
        arrived(in2.at[k], two_recv.at[k])
    total = in2[0].astype(jnp.float32)
    for k in range(1, PLANES):
        total += in2[k].astype(jnp.float32)
    dq_ref[...] = (total * scale).T.astype(dq_ref.dtype)

    for side in range(2):
        here = jnp.logical_and(on_self, xh == side)

        @pl.when(jnp.logical_not(here))
        def _():
            first(side).wait_send()

    for k in range(PLANES):
        for s in range(2):
            for copy in onward(k, s):
                copy.wait_send()
            to_sibling(k, s).wait_send()
        for b in range(4):
            here, copy = spread(k, b)
            pl.when(jnp.logical_not(here))(copy.wait_send)
        here, copy = home(k)
        pl.when(jnp.logical_not(here))(copy.wait_send)


def per_device(queries, grad_out, outputs, log_sums, prompt_keys, prompt_values):
    rows, dim = queries.shape[2:]
    positions, groups = prompt_keys.shape[:2]
    vmem = pl.BlockSpec(memory_space=pltpu.VMEM)
    hbm = pl.BlockSpec(memory_space=pl.ANY)
    dma = pltpu.SemaphoreType.DMA
    low, full = jnp.bfloat16, jnp.float32
    dq, dk, dv = pl.pallas_call(
        kernel,
        out_shape=(
            jax.ShapeDtypeStruct((rows, dim), low),
            jax.ShapeDtypeStruct((positions, dim), low),
            jax.ShapeDtypeStruct((positions, dim), low),
        ),
        in_specs=[vmem] * 4 + [hbm] * 2,
        out_specs=(vmem,) * 3,
        scratch_shapes=[
            pltpu.VMEM((2 * rows + 16, dim), low),
            pltpu.VMEM((PLANES, 2, 2, 2 * rows + 16, dim), low),
            pltpu.VMEM((PLANES, 4, dim, rows), low),
            pltpu.VMEM((PLANES, 4, dim, rows), low),
            pltpu.VMEM((PLANES, dim, rows), low),
            pltpu.VMEM((PLANES, dim, rows), low),
            pltpu.VMEM((positions * groups, dim), low),
            pltpu.VMEM((positions * groups, dim), low),
            pltpu.VMEM((positions, dim), low),
            pltpu.VMEM((positions, dim), low),
            pltpu.VMEM((dim, positions), low),
            pltpu.VMEM((positions, dim), full),
            pltpu.VMEM((positions, dim), full),
            dma((2,)), dma((2,)), dma((2,)),
            dma((PLANES, 2)), dma((PLANES, 2)), dma((PLANES, 2)),
            dma((PLANES, 2)), dma((PLANES, 2)),
            dma((PLANES, 4)), dma((PLANES, 4)), dma((PLANES,)), dma((PLANES,)),
        ],
        compiler_params=pltpu.CompilerParams(
            collective_id=0, has_side_effects=True, vmem_limit_bytes=60 << 20
        ),
    )(
        queries[0, 0], grad_out[0, 0], outputs[0, 0], log_sums[0],
        prompt_keys.reshape(positions * groups, dim), prompt_values.reshape(positions * groups, dim),
    )
    return dq[None, None], dk[:, None, :], dv[:, None, :]


def solution(mesh):
    in_specs = (
        P("resp", "seq", None, None),
        P("resp", "seq", None, None),
        P("resp", "seq", None, None),
        P("resp", "seq", None),
        P("seq", None, None),
        P("seq", None, None),
    )
    out_specs = (P("resp", "seq", None, None), P("seq", "resp", None), P("seq", "resp", None))
    return jax.shard_map(
        per_device, mesh=mesh, in_specs=in_specs, out_specs=out_specs, check_vma=False
    )
```

time: 251 us -> 64.7 us (0.26)
  the two profiles are of different devices: /device:TPU:16 before, /device:TPU:8 now
where the time goes in v2:
time: 64.7 us; the launch traced here: 64.4 us
  Pallas kernels  59 us (91%)
  local copies, waits for them, and re-layouts  4.71 us (7%)
    pallas_call x1, Pallas kernels, per_device(): pl.pallas_call(kernel, out_shape=(jax.ShapeDtypeStruct((rows, dim), low),...  59 us
    unnamed x3, local copies, waits for them, and re-layouts  4.71 us

profile of v2, /device:TPU:8, one launch (start us, length us, event | category | flops | bytes accessed | tf_op | source)
XLA Modules:
  0.0 64.4 jit_solution(13492604708301460465)
XLA Ops:
  0.6 59.0 %shard_map.85 = (bf16[128,128]{1,0:T(8,128)(2,1)}, bf16[1024,128]{1,0:T(8,128)(2,1)}, bf16[1024,128]{1,0:T(8,128)(2,1)}) custom-call(bf16[128,128]{1,0:T(8,128)(2,1)} %bitcast.13, bf16[128,128]{1,0:T(8,128)(2,1)} %bitcast.14, bf16[128,128]{1,0:T(8,128)(2,1)} %bitcast.15, f32[1,128]{1,0:T(1,128)} %bitcast.17, bf16[8192,128]{1,0:T(8,128)(2,1)} %bitcast.9, ...), custom_call_target="tpu_custom_call" | custom-call | tf_op jit(solution)/shard_map/pallas_call | solution.py:286
  59.7 1.4 %copy.12 = bf16[1,1,128,128]{3,2,1,0:T(8,128)(2,1)} copy(bf16[1,1,128,128]{3,2,1,0:T(8,128)(2,1)} %bitcast.16) | data formatting | bytes 65536
  61.1 1.7 %copy.13 = bf16[1024,1,128]{2,0,1:T(8,128)(2,1)} copy(bf16[1024,1,128]{2,0,1:T(8,128)(2,1)} %bitcast.12) | data formatting | bytes 524288
  62.7 1.7 %copy.14 = bf16[1024,1,128]{2,0,1:T(8,128)(2,1)} copy(bf16[1024,1,128]{2,0,1:T(8,128)(2,1)} %bitcast.11) | data formatting | bytes 524288

commit v3 on v2

v3 whole, which is shorter than its diff:
```python
import functools

import jax
import jax.numpy as jnp
from jax import lax
from jax.experimental import pallas as pl
from jax.experimental.pallas import tpu as pltpu
from jax.sharding import PartitionSpec as P

NT = (((1,), (1,)), ((), ()))
NN = (((1,), (0,)), ((), ()))
MESH = pl.DeviceIdType.MESH
LOG2E = 1.4426950408889634
STEP = 512
PLANES = 8
AHEAD = 5
WINDOW = 3
LAG = 4


def split3(row):
    high = row.astype(jnp.bfloat16).astype(jnp.float32)
    rest = row - high
    mid = rest.astype(jnp.bfloat16).astype(jnp.float32)
    return [high, mid, rest - mid]


def kernel(
    q_ref, g_ref, o_ref, sums_ref, k_hbm, v_hbm,
    dq_ref, dk_ref, dv_ref,
    pack, held, blk, part, other, pair, in1, mid, in2, k_all, v_all, keys, values, keys_t, acc_k, acc_v,
    kv_sem, held_send, held_recv, blk_send, blk_recv, sib_send, sib_recv, core_send, core_recv,
    one_send, one_recv, two_send, two_recv,
):
    seq, grp = lax.axis_index("seq"), lax.axis_index("resp")
    z, j = seq // 4, lax.rem(seq, 4)
    xh, core = j // 2, lax.rem(j, 2)
    rows = q_ref.shape[0]
    positions = dk_ref.shape[0]
    groups = k_all.shape[0] // positions
    scale = q_ref.shape[1] ** -0.5
    sibling = z * 4 + 2 * xh + (1 - core)

    def wrap(value):
        return lax.rem(value + 2 * PLANES, PLANES)

    def remote(src, dst, send, recv, seq_to, resp_to):
        return pltpu.make_async_remote_copy(
            src_ref=src, dst_ref=dst, send_sem=send, recv_sem=recv,
            device_id=(seq_to, resp_to), device_id_type=MESH,
        )

    def arrived(ref, sem):
        pltpu.make_async_copy(ref, ref, sem).wait()

    load_k = pltpu.make_async_copy(k_hbm, k_all, kv_sem.at[0])
    load_v = pltpu.make_async_copy(v_hbm, v_all, kv_sem.at[1])
    load_k.start()
    load_v.start()

    barrier = pltpu.get_barrier_semaphore()

    @pl.loop(1, PLANES)
    def _(t):
        pl.semaphore_signal(
            barrier, inc=1, device_id=(lax.rem(z + t, PLANES) * 4 + j, grp), device_id_type=MESH
        )

    @pl.loop(1, 2 * PLANES)
    def _(t):
        peer = lax.rem(grp * 2 + xh + t, 2 * PLANES)
        pl.semaphore_signal(
            barrier, inc=1, device_id=(z * 4 + 2 * lax.rem(peer, 2) + core, peer // 2),
            device_id_type=MESH,
        )

    pl.semaphore_signal(barrier, inc=1, device_id=(sibling, grp), device_id_type=MESH)

    grad_own = g_ref[...]
    product = grad_own.astype(jnp.float32) * o_ref[...].astype(jnp.float32)
    delta = jnp.sum(product.T, axis=0, keepdims=True)
    stats = split3(sums_ref[...] * LOG2E) + split3(delta)
    stats = jnp.concatenate(stats + [jnp.zeros((10, rows), jnp.float32)], axis=0)
    pack[0:rows, :] = q_ref[...]
    pack[rows : 2 * rows, :] = grad_own
    pack[2 * rows :, :] = stats.astype(jnp.bfloat16)

    pl.semaphore_wait(barrier, PLANES - 1 + 2 * PLANES - 1 + 1)

    def move(here, copy, src, dst, recv):
        pl.when(here)(lambda: pltpu.make_async_copy(src, dst, recv).start())
        pl.when(jnp.logical_not(here))(lambda: copy.start())

    def along(k):
        plane = wrap(z + grp + k)
        return plane == z, remote(
            pack, held.at[k], held_send.at[k], held_recv.at[k], plane * 4 + j, grp
        )

    def launch(k):
        here, copy = along(k)
        move(here, copy, pack, held.at[k], held_recv.at[k])

    for k in range(WINDOW):
        launch(k)

    def across(k, side):
        head = wrap(z - grp - k)
        return jnp.logical_and(head == grp, xh == side), remote(
            held.at[k], blk.at[k, core, xh], blk_send.at[k, side], blk_recv.at[k, xh],
            z * 4 + 2 * side + core, head,
        )

    def forward(k):
        arrived(held.at[k], held_recv.at[k])
        for side in range(2):
            here, copy = across(k, side)
            move(here, copy, held.at[k], blk.at[k, core, xh], blk_recv.at[k, xh])

    def to_sibling(k):
        return remote(blk.at[k, core], blk.at[k, core], sib_send.at[k], sib_recv.at[k], sibling, grp)

    def share(k):
        for s in range(2):
            arrived(blk.at[k, core, s], blk_recv.at[k, s])
        to_sibling(k).start()

    load_k.wait()
    load_v.wait()
    tile = 128
    pick = (
        lax.broadcasted_iota(jnp.int32, (tile, tile * groups), 1)
        == lax.broadcasted_iota(jnp.int32, (tile, tile * groups), 0) * groups + grp
    ).astype(jnp.bfloat16)
    for t in range(positions // tile):
        wide, narrow = pl.ds(t * tile * groups, tile * groups), pl.ds(t * tile, tile)
        keys[narrow, :] = lax.dot_general(
            pick, k_all[wide, :], NN, preferred_element_type=jnp.float32
        ).astype(jnp.bfloat16)
        values[narrow, :] = lax.dot_general(
            pick, v_all[wide, :], NN, preferred_element_type=jnp.float32
        ).astype(jnp.bfloat16)
    keys_t[...] = keys[...].T
    acc_k[...] = jnp.zeros_like(acc_k)
    acc_v[...] = jnp.zeros_like(acc_v)

    def work(k):
        parts = [blk.at[k, b // 2, b % 2] for b in range(4)]
        query = jnp.concatenate([p[0:rows, :] for p in parts], axis=0)
        grad = jnp.concatenate([p[rows : 2 * rows, :] for p in parts], axis=0)
        stats = [p[2 * rows :, :].astype(jnp.float32) for p in parts]
        sums = jnp.concatenate([s[0:1] + s[1:2] + s[2:3] for s in stats], axis=1)
        delta = jnp.concatenate([s[3:4] + s[4:5] + s[5:6] for s in stats], axis=1)
        total = None
        for at in range(0, positions, STEP):
            span = pl.ds(at, STEP)
            scores = lax.dot_general(keys[span, :], query, NT, preferred_element_type=jnp.float32)
            probs = lax.dot_general(values[span, :], grad, NT, preferred_element_type=jnp.float32)
            weights = jnp.exp2(scores * (scale * LOG2E) - sums)
            low = weights.astype(jnp.bfloat16)
            grad_scores = (weights * (probs - delta)).astype(jnp.bfloat16)
            acc_v[span, :] += lax.dot_general(low, grad, NN, preferred_element_type=jnp.float32)
            acc_k[span, :] += lax.dot_general(grad_scores, query, NN, preferred_element_type=jnp.float32)
            term = lax.dot_general(keys_t[:, span], grad_scores, NN, preferred_element_type=jnp.float32)
            total = term if total is None else total + term
        total = total.astype(jnp.bfloat16)
        for b in range(4):
            part[k, b // 2, b % 2] = total[:, b * rows : (b + 1) * rows]

    def to_core(k):
        return remote(
            part.at[k, 1 - core], other.at[k], core_send.at[k], core_recv.at[k], sibling, grp
        )

    def spread(k, s):
        place = wrap(z - grp - k)
        return jnp.logical_and(place == grp, xh == s), remote(
            pair.at[k, s], in1.at[k, xh], one_send.at[k, s], one_recv.at[k, xh],
            z * 4 + 2 * s + core, place,
        )

    def add_cores(k):
        arrived(other.at[k], core_recv.at[k])
        for s in range(2):
            pair[k, s] = (
                part[k, core, s].astype(jnp.float32) + other[k, s].astype(jnp.float32)
            ).astype(jnp.bfloat16)
            here, copy = spread(k, s)
            move(here, copy, pair.at[k, s], in1.at[k, xh], one_recv.at[k, xh])

    def home(k):
        plane = wrap(z - grp - k)
        return plane == z, remote(
            mid.at[k], in2.at[k], two_send.at[k], two_recv.at[k], plane * 4 + j, grp
        )

    def add_plane(k):
        for s in range(2):
            arrived(in1.at[k, s], one_recv.at[k, s])
        mid[k] = (in1[k, 0].astype(jnp.float32) + in1[k, 1].astype(jnp.float32)).astype(jnp.bfloat16)
        here, copy = home(k)
        move(here, copy, mid.at[k], in2.at[k], two_recv.at[k])

    def left(here, copy):
        pl.when(jnp.logical_not(here))(lambda: copy.wait_send())

    for k in range(WINDOW, PLANES):
        left(*along(k - WINDOW))
        launch(k)
        if k >= LAG:
            forward(k - LAG)
    for k in range(PLANES - LAG, AHEAD):
        forward(k)
    share(0)
    for k in range(PLANES):
        if k + AHEAD < PLANES:
            forward(k + AHEAD)
        if k + 1 < PLANES:
            share(k + 1)
        arrived(blk.at[k, 1 - core], sib_recv.at[k])
        work(k)
        to_core(k).start()
        if k >= 1:
            add_cores(k - 1)
        if k >= 4:
            add_plane(k - 4)
    add_cores(PLANES - 1)
    dk_ref[...] = (acc_k[...] * scale).astype(dk_ref.dtype)
    dv_ref[...] = acc_v[...].astype(dv_ref.dtype)
    for k in range(PLANES - 4, PLANES):
        add_plane(k)
    total = jnp.zeros((q_ref.shape[1], rows), jnp.float32)
    for k in range(PLANES):
        arrived(in2.at[k], two_recv.at[k])
        total += in2[k].astype(jnp.float32)
    dq_ref[...] = (total * scale).T.astype(dq_ref.dtype)

    for k in range(PLANES - WINDOW, PLANES):
        left(*along(k))
    for k in range(PLANES):
        for s in range(2):
            left(*across(k, s))
            left(*spread(k, s))
        to_sibling(k).wait_send()
        to_core(k).wait_send()
        left(*home(k))


def copy_kernel(*refs):
    half = len(refs) // 2
    for src, dst in zip(refs[:half], refs[half:]):
        dst[...] = src[...]


def per_device(queries, grad_out, outputs, log_sums, prompt_keys, prompt_values):
    rows, dim = queries.shape[2:]
    positions, groups = prompt_keys.shape[:2]
    vmem = pl.BlockSpec(memory_space=pltpu.VMEM)
    hbm = pl.BlockSpec(memory_space=pl.ANY)
    dma = pltpu.SemaphoreType.DMA
    low, full = jnp.bfloat16, jnp.float32
    dq, dk, dv = pl.pallas_call(
        kernel,
        out_shape=(
            jax.ShapeDtypeStruct((rows, dim), low),
            jax.ShapeDtypeStruct((positions, dim), low),
            jax.ShapeDtypeStruct((positions, dim), low),
        ),
        in_specs=[vmem] * 4 + [hbm] * 2,
        out_specs=(vmem,) * 3,
        scratch_shapes=[
            pltpu.VMEM((2 * rows + 16, dim), low),
            pltpu.VMEM((PLANES, 2 * rows + 16, dim), low),
            pltpu.VMEM((PLANES, 2, 2, 2 * rows + 16, dim), low),
            pltpu.VMEM((PLANES, 2, 2, dim, rows), low),
            pltpu.VMEM((PLANES, 2, dim, rows), low),
            pltpu.VMEM((PLANES, 2, dim, rows), low),
            pltpu.VMEM((PLANES, 2, dim, rows), low),
            pltpu.VMEM((PLANES, dim, rows), low),
            pltpu.VMEM((PLANES, dim, rows), low),
            pltpu.VMEM((positions * groups, dim), low),
            pltpu.VMEM((positions * groups, dim), low),
            pltpu.VMEM((positions, dim), low),
            pltpu.VMEM((positions, dim), low),
            pltpu.VMEM((dim, positions), low),
            pltpu.VMEM((positions, dim), full),
            pltpu.VMEM((positions, dim), full),
            dma((2,)), dma((PLANES,)), dma((PLANES,)),
            dma((PLANES, 2)), dma((PLANES, 2)), dma((PLANES,)), dma((PLANES,)),
            dma((PLANES,)), dma((PLANES,)),
            dma((PLANES, 2)), dma((PLANES, 2)), dma((PLANES,)), dma((PLANES,)),
        ],
        compiler_params=pltpu.CompilerParams(
            collective_id=0, has_side_effects=True, vmem_limit_bytes=60 << 20
        ),
    )(
        queries[0, 0], grad_out[0, 0], outputs[0, 0], log_sums[0],
        prompt_keys.reshape(positions * groups, dim), prompt_values.reshape(positions * groups, dim),
    )
    outs = (dq, dk, dv)
    dq, dk, dv = pl.pallas_call(
        copy_kernel,
        out_shape=tuple(jax.ShapeDtypeStruct(x.shape, x.dtype) for x in outs),
        in_specs=[vmem] * 3,
        out_specs=(vmem,) * 3,
    )(*outs)
    return dq[None, None], dk[:, None, :], dv[:, None, :]


def solution(mesh):
    in_specs = (
        P("resp", "seq", None, None),
        P("resp", "seq", None, None),
        P("resp", "seq", None, None),
        P("resp", "seq", None),
        P("seq", None, None),
        P("seq", None, None),
    )
    out_specs = (P("resp", "seq", None, None), P("seq", "resp", None), P("seq", "resp", None))
    return jax.shard_map(
        per_device, mesh=mesh, in_specs=in_specs, out_specs=out_specs, check_vma=False
    )
```

time: 64.7 us -> 59.6 us (0.921)
  the two profiles are of different devices: /device:TPU:8 before, /device:TPU:1 now
where the time goes in v3:
time: 59.6 us; the launch traced here: 59.4 us
  Pallas kernels  58.8 us (99%)
  between operations  0.64 us (1%)
    pallas_call x1, Pallas kernels, per_device(): pl.pallas_call(kernel, out_shape=(jax.ShapeDtypeStruct((rows, dim), low),...  56.9 us
    pallas_call x1, Pallas kernels, per_device(): pl.pallas_call(copy_kernel, out_shape=tuple((jax.ShapeDtypeStruct(x.shape...  1.87 us

profile of v3, /device:TPU:1, one launch (start us, length us, event | category | flops | bytes accessed | tf_op | source)
XLA Modules:
  0.0 59.4 jit_solution(14317490445391114863)
XLA Ops:
  0.6 56.9 %shard_map.85 = (bf16[128,128]{1,0:T(8,128)(2,1)}, bf16[1024,128]{1,0:T(8,128)(2,1)}, bf16[1024,128]{1,0:T(8,128)(2,1)}) custom-call(bf16[128,128]{1,0:T(8,128)(2,1)} %bitcast.11, bf16[128,128]{1,0:T(8,128)(2,1)} %bitcast.12, bf16[128,128]{1,0:T(8,128)(2,1)} %bitcast.13, f32[1,128]{1,0:T(1,128)} %bitcast.14, bf16[8192,128]{1,0:T(8,128)(2,1)} %bitcast.9, ...), custom_call_target="tpu_custom_call" | custom-call | tf_op jit(solution)/shard_map/pallas_call | solution.py:262
  57.5 1.9 %shard_map.86 = (bf16[128,128]{1,0:T(8,128)(2,1)}, bf16[1024,128]{1,0:T(8,128)(2,1)}, bf16[1024,128]{1,0:T(8,128)(2,1)}) custom-call(bf16[128,128]{1,0:T(8,128)(2,1)} %get-tuple-element.9.refs_0_, bf16[1024,128]{1,0:T(8,128)(2,1)} %get-tuple-element.10.refs_1_, bf16[1024,128]{1,0:T(8,128)(2,1)} %get-tuple-element.11.refs_2_), custom_call_target="tpu_custom_call" | custom-call | tf_op jit(solution)/shard_map/pallas_call | solution.py:301

commit v4 on v3

--- a/solution.py
+++ b/solution.py
@@ -13,9 +13,39 @@
 LOG2E = 1.4426950408889634
 STEP = 512
 PLANES = 8
+SPREAD = (4, 3, 6)
+ORDER = (2, 5, 0, 4, 7, 3, 1, 6)
 AHEAD = 5
-WINDOW = 3
-LAG = 4
+WINDOW = 8
+
+
+def times(columns, value):
+    return functools.reduce(lambda x, y: x ^ y, [c for i, c in enumerate(columns) if value >> i & 1], 0)
+
+
+def inverse(columns):
+    return tuple(next(v for v in range(PLANES) if times(columns, v) == 1 << i) for i in range(3))
+
+
+def mapped(first, a, second, b, constant):
+    total = 0
+    for i in range(3):
+        bit = constant >> i & 1
+        for columns, value in ((first, a), (second, b)):
+            for n, column in enumerate(columns):
+                if column >> i & 1:
+                    bit = bit + value[n]
+        total = total + lax.rem(bit, 2) * (1 << i)
+    return total
+
+
+def joined(one, two):
+    return tuple(x ^ y for x, y in zip(one, two))
+
+
+SAME = (1, 2, 4)
+REST = joined(SPREAD, SAME)
+BACK, UNDO = inverse(SPREAD), inverse(REST)
 
 
 def split3(row):
@@ -26,23 +56,33 @@
 
 
 def kernel(
-    q_ref, g_ref, o_ref, sums_ref, k_hbm, v_hbm,
+    q_hbm, g_hbm, o_hbm, sums_hbm, k_hbm, v_hbm,
     dq_ref, dk_ref, dv_ref,
-    pack, held, blk, part, other, pair, in1, mid, in2, k_all, v_all, keys, values, keys_t, acc_k, acc_v,
+    pack, held, blk, part, other, pair, in1, mid, in2, last, k_all, v_all, keys, values, keys_t, acc_k, acc_v,
     kv_sem, held_send, held_recv, blk_send, blk_recv, sib_send, sib_recv, core_send, core_recv,
-    one_send, one_recv, two_send, two_recv,
+    one_send, one_recv, two_send, two_recv, last_send, last_recv, out_sem, own_sem, o_own, sums_own,
 ):
     seq, grp = lax.axis_index("seq"), lax.axis_index("resp")
     z, j = seq // 4, lax.rem(seq, 4)
     xh, core = j // 2, lax.rem(j, 2)
-    rows = q_ref.shape[0]
+    rows = q_hbm.shape[0]
     positions = dk_ref.shape[0]
     groups = k_all.shape[0] // positions
-    scale = q_ref.shape[1] ** -0.5
+    scale = q_hbm.shape[1] ** -0.5
     sibling = z * 4 + 2 * xh + (1 - core)
 
-    def wrap(value):
-        return lax.rem(value + 2 * PLANES, PLANES)
+    bits_z = [lax.rem(z, 2), lax.rem(z // 2, 2), z // 4]
+    bits_g = [lax.rem(grp, 2), lax.rem(grp // 2, 2), grp // 4]
+
+    def place_of(k):
+        return mapped(SPREAD, bits_z, REST, bits_g, ORDER[k])
+
+    def plane_of(k):
+        return mapped(joined(BACK, SAME), bits_z, BACK, bits_g, times(BACK, ORDER[k]))
+
+    def head_of(k):
+        both = tuple(times(UNDO, c) for c in SPREAD)
+        return mapped(both, bits_z, UNDO, bits_g, times(UNDO, ORDER[k]))
 
     def remote(src, dst, send, recv, seq_to, resp_to):
         return pltpu.make_async_remote_copy(
@@ -53,6 +93,14 @@
     def arrived(ref, sem):
         pltpu.make_async_copy(ref, ref, sem).wait()
 
+    own = [
+        pltpu.make_async_copy(src, dst, own_sem.at[i])
+        for i, (src, dst) in enumerate((
+            (g_hbm, pack.at[rows : 2 * rows]), (o_hbm, o_own), (sums_hbm, sums_own), (q_hbm, pack.at[0:rows]),
+        ))
+    ]
+    for load in own:
+        load.start()
     load_k = pltpu.make_async_copy(k_hbm, k_all, kv_sem.at[0])
     load_v = pltpu.make_async_copy(v_hbm, v_all, kv_sem.at[1])
     load_k.start()
@@ -75,24 +123,28 @@
         )
 
     pl.semaphore_signal(barrier, inc=1, device_id=(sibling, grp), device_id_type=MESH)
-
-    grad_own = g_ref[...]
-    product = grad_own.astype(jnp.float32) * o_ref[...].astype(jnp.float32)
+    for side in range(2):
+        pl.semaphore_signal(
+            barrier, inc=1, device_id=(z * 4 + 2 * side + 1 - core, head_of(PLANES - 1)),
+            device_id_type=MESH,
+        )
+
+    for load in own:
+        load.wait()
+    product = pack[rows : 2 * rows, :].astype(jnp.float32) * o_own[...].astype(jnp.float32)
     delta = jnp.sum(product.T, axis=0, keepdims=True)
-    stats = split3(sums_ref[...] * LOG2E) + split3(delta)
+    stats = split3(sums_own[...] * LOG2E) + split3(delta)
     stats = jnp.concatenate(stats + [jnp.zeros((10, rows), jnp.float32)], axis=0)
-    pack[0:rows, :] = q_ref[...]
-    pack[rows : 2 * rows, :] = grad_own
     pack[2 * rows :, :] = stats.astype(jnp.bfloat16)
 
-    pl.semaphore_wait(barrier, PLANES - 1 + 2 * PLANES - 1 + 1)
+    pl.semaphore_wait(barrier, PLANES - 1 + 2 * PLANES - 1 + 1 + 2)
 
     def move(here, copy, src, dst, recv):
         pl.when(here)(lambda: pltpu.make_async_copy(src, dst, recv).start())
         pl.when(jnp.logical_not(here))(lambda: copy.start())
 
     def along(k):
-        plane = wrap(z + grp + k)
+        plane = plane_of(k)
         return plane == z, remote(
             pack, held.at[k], held_send.at[k], held_recv.at[k], plane * 4 + j, grp
         )
@@ -105,7 +157,7 @@
         launch(k)
 
     def across(k, side):
-        head = wrap(z - grp - k)
+        head = head_of(k)
         return jnp.logical_and(head == grp, xh == side), remote(
             held.at[k], blk.at[k, core, xh], blk_send.at[k, side], blk_recv.at[k, xh],
             z * 4 + 2 * side + core, head,
@@ -173,7 +225,7 @@
         )
 
     def spread(k, s):
-        place = wrap(z - grp - k)
+        place = place_of(k)
         return jnp.logical_and(place == grp, xh == s), remote(
             pair.at[k, s], in1.at[k, xh], one_send.at[k, s], one_recv.at[k, xh],
             z * 4 + 2 * s + core, place,
@@ -189,27 +241,36 @@
             move(here, copy, pair.at[k, s], in1.at[k, xh], one_recv.at[k, xh])
 
     def home(k):
-        plane = wrap(z - grp - k)
+        plane = head_of(k)
         return plane == z, remote(
             mid.at[k], in2.at[k], two_send.at[k], two_recv.at[k], plane * 4 + j, grp
         )
 
     def add_plane(k):
-        for s in range(2):
-            arrived(in1.at[k, s], one_recv.at[k, s])
-        mid[k] = (in1[k, 0].astype(jnp.float32) + in1[k, 1].astype(jnp.float32)).astype(jnp.bfloat16)
+        if k < PLANES - 1:
+            terms = [(in1.at[k, s], one_recv.at[k, s]) for s in range(2)]
+        else:
+            terms = [(last.at[s], last_recv.at[s]) for s in range(4)]
+        total = None
+        for ref, sem in terms:
+            arrived(ref, sem)
+            term = ref[...].astype(jnp.float32)
+            total = term if total is None else total + term
+        mid[k] = total.astype(jnp.bfloat16)
         here, copy = home(k)
         move(here, copy, mid.at[k], in2.at[k], two_recv.at[k])
 
+    def spread_last(b):
+        place, owner = place_of(PLANES - 1), (b % 2) * 2 + b // 2
+        return jnp.logical_and(place == grp, owner == j), remote(
+            part.at[PLANES - 1, b // 2, b % 2], last.at[j], last_send.at[b], last_recv.at[j],
+            z * 4 + owner, place,
+        )
+
     def left(here, copy):
         pl.when(jnp.logical_not(here))(lambda: copy.wait_send())
 
-    for k in range(WINDOW, PLANES):
-        left(*along(k - WINDOW))
-        launch(k)
-        if k >= LAG:
-            forward(k - LAG)
-    for k in range(PLANES - LAG, AHEAD):
+    for k in range(AHEAD):
         forward(k)
     share(0)
     for k in range(PLANES):
@@ -219,17 +280,27 @@
             share(k + 1)
         arrived(blk.at[k, 1 - core], sib_recv.at[k])
         work(k)
-        to_core(k).start()
+        if k < PLANES - 1:
+            to_core(k).start()
+        else:
+            for b in range(4):
+                here, copy = spread_last(b)
+                move(here, copy, part.at[k, b // 2, b % 2], last.at[j], last_recv.at[j])
         if k >= 1:
             add_cores(k - 1)
         if k >= 4:
             add_plane(k - 4)
-    add_cores(PLANES - 1)
-    dk_ref[...] = (acc_k[...] * scale).astype(dk_ref.dtype)
-    dv_ref[...] = acc_v[...].astype(dv_ref.dtype)
+    keys[...] = (acc_k[...] * scale).astype(keys.dtype)
+    values[...] = acc_v[...].astype(values.dtype)
+    outs = [
+        pltpu.make_async_copy(keys, dk_ref, out_sem.at[0]),
+        pltpu.make_async_copy(values, dv_ref, out_sem.at[1]),
+    ]
+    for out in outs:
+        out.start()
     for k in range(PLANES - 4, PLANES):
         add_plane(k)
-    total = jnp.zeros((q_ref.shape[1], rows), jnp.float32)
+    total = jnp.zeros((q_hbm.shape[1], rows), jnp.float32)
     for k in range(PLANES):
         arrived(in2.at[k], two_recv.at[k])
         total += in2[k].astype(jnp.float32)
@@ -240,10 +311,16 @@
     for k in range(PLANES):
         for s in range(2):
             left(*across(k, s))
-            left(*spread(k, s))
         to_sibling(k).wait_send()
-        to_core(k).wait_send()
         left(*home(k))
+        if k < PLANES - 1:
+            for s in range(2):
+                left(*spread(k, s))
+            to_core(k).wait_send()
+    for b in range(4):
+        left(*spread_last(b))
+    for out in outs:
+        out.wait()
 
 
 def copy_kernel(*refs):
@@ -266,8 +343,8 @@
             jax.ShapeDtypeStruct((positions, dim), low),
             jax.ShapeDtypeStruct((positions, dim), low),
         ),
-        in_specs=[vmem] * 4 + [hbm] * 2,
-        out_specs=(vmem,) * 3,
+        in_specs=[hbm] * 6,
+        out_specs=(vmem, hbm, hbm),
         scratch_shapes=[
             pltpu.VMEM((2 * rows + 16, dim), low),
             pltpu.VMEM((PLANES, 2 * rows + 16, dim), low),
@@ -278,6 +355,7 @@
             pltpu.VMEM((PLANES, 2, dim, rows), low),
             pltpu.VMEM((PLANES, dim, rows), low),
             pltpu.VMEM((PLANES, dim, rows), low),
+            pltpu.VMEM((4, dim, rows), low),
             pltpu.VMEM((positions * groups, dim), low),
             pltpu.VMEM((positions * groups, dim), low),
             pltpu.VMEM((positions, dim), low),
@@ -289,6 +367,8 @@
             dma((PLANES, 2)), dma((PLANES, 2)), dma((PLANES,)), dma((PLANES,)),
             dma((PLANES,)), dma((PLANES,)),
             dma((PLANES, 2)), dma((PLANES, 2)), dma((PLANES,)), dma((PLANES,)),
+            dma((4,)), dma((4,)), dma((2,)), dma((4,)),
+            pltpu.VMEM((rows, dim), low), pltpu.VMEM((1, rows), full),
         ],
         compiler_params=pltpu.CompilerParams(
             collective_id=0, has_side_effects=True, vmem_limit_bytes=60 << 20

time: 59.6 us -> 58 us (0.973)
  the two profiles are of different devices: /device:TPU:1 before, /device:TPU:16 now
where the time goes in v4:
time: 58 us; the launch traced here: 57.2 us
  Pallas kernels  56.5 us (97%)
  between operations  0.64 us (1%)
    pallas_call x1, Pallas kernels, per_device(): pl.pallas_call(kernel, out_shape=(jax.ShapeDtypeStruct((rows, dim), low),...  54.7 us
    pallas_call x1, Pallas kernels, per_device(): pl.pallas_call(copy_kernel, out_shape=tuple((jax.ShapeDtypeStruct(x.shape...  1.87 us

profile of v4, /device:TPU:16, one launch (start us, length us, event | category | flops | bytes accessed | tf_op | source)
XLA Modules:
  0.0 57.2 jit_solution(16619115146006171473)
XLA Ops:
  0.6 54.7 %shard_map.85 = (bf16[128,128]{1,0:T(8,128)(2,1)}, bf16[1024,128]{1,0:T(8,128)(2,1)}, bf16[1024,128]{1,0:T(8,128)(2,1)}) custom-call(bf16[128,128]{1,0:T(8,128)(2,1)} %bitcast.11, bf16[128,128]{1,0:T(8,128)(2,1)} %bitcast.12, bf16[128,128]{1,0:T(8,128)(2,1)} %bitcast.13, f32[1,128]{1,0:T(1,128)} %bitcast.14, bf16[8192,128]{1,0:T(8,128)(2,1)} %bitcast.9, ...), custom_call_target="tpu_custom_call" | custom-call | tf_op jit(solution)/shard_map/pallas_call | solution.py:339
  55.3 1.9 %shard_map.86 = (bf16[128,128]{1,0:T(8,128)(2,1)}, bf16[1024,128]{1,0:T(8,128)(2,1)}, bf16[1024,128]{1,0:T(8,128)(2,1)}) custom-call(bf16[128,128]{1,0:T(8,128)(2,1)} %get-tuple-element.9.refs_0_, bf16[1024,128]{1,0:T(8,128)(2,1)} %get-tuple-element.10.refs_1_, bf16[1024,128]{1,0:T(8,128)(2,1)} %get-tuple-element.11.refs_2_), custom_call_target="tpu_custom_call" | custom-call | tf_op jit(solution)/shard_map/pallas_call | solution.py:381

commit v5 on v4

--- a/solution.py
+++ b/solution.py
@@ -60,7 +60,7 @@
     dq_ref, dk_ref, dv_ref,
     pack, held, blk, part, other, pair, in1, mid, in2, last, k_all, v_all, keys, values, keys_t, acc_k, acc_v,
     kv_sem, held_send, held_recv, blk_send, blk_recv, sib_send, sib_recv, core_send, core_recv,
-    one_send, one_recv, two_send, two_recv, last_send, last_recv, out_sem, own_sem, o_own, sums_own,
+    one_send, one_recv, two_send, two_recv, last_send, last_recv, out_sem, own_sem, near_send, o_own, sums_own,
 ):
     seq, grp = lax.axis_index("seq"), lax.axis_index("resp")
     z, j = seq // 4, lax.rem(seq, 4)
@@ -149,9 +149,21 @@
             pack, held.at[k], held_send.at[k], held_recv.at[k], plane * 4 + j, grp
         )
 
+    slot = sum(k * (head_of(k) == z).astype(jnp.int32) for k in range(PLANES))
+
+    def near(side):
+        return jnp.logical_and(z == grp, xh == side), remote(
+            pack, blk.at[slot, core, xh], near_send.at[side], blk_recv.at[slot, xh],
+            z * 4 + 2 * side + core, z,
+        )
+
+    for side in range(2):
+        here, copy = near(side)
+        move(here, copy, pack, blk.at[slot, core, xh], blk_recv.at[slot, xh])
+
     def launch(k):
         here, copy = along(k)
-        move(here, copy, pack, held.at[k], held_recv.at[k])
+        pl.when(jnp.logical_not(here))(lambda: copy.start())
 
     for k in range(WINDOW):
         launch(k)
@@ -164,10 +176,12 @@
         )
 
     def forward(k):
-        arrived(held.at[k], held_recv.at[k])
-        for side in range(2):
-            here, copy = across(k, side)
-            move(here, copy, held.at[k], blk.at[k, core, xh], blk_recv.at[k, xh])
+        @pl.when(head_of(k) != z)
+        def _():
+            arrived(held.at[k], held_recv.at[k])
+            for side in range(2):
+                here, copy = across(k, side)
+                move(here, copy, held.at[k], blk.at[k, core, xh], blk_recv.at[k, xh])
 
     def to_sibling(k):
         return remote(blk.at[k, core], blk.at[k, core], sib_send.at[k], sib_recv.at[k], sibling, grp)
@@ -310,7 +324,8 @@
         left(*along(k))
     for k in range(PLANES):
         for s in range(2):
-            left(*across(k, s))
+            here, copy = across(k, s)
+            left(jnp.logical_or(here, head_of(k) == z), copy)
         to_sibling(k).wait_send()
         left(*home(k))
         if k < PLANES - 1:
@@ -319,6 +334,8 @@
             to_core(k).wait_send()
     for b in range(4):
         left(*spread_last(b))
+    for side in range(2):
+        left(*near(side))
     for out in outs:
         out.wait()
 
@@ -367,7 +384,7 @@
             dma((PLANES, 2)), dma((PLANES, 2)), dma((PLANES,)), dma((PLANES,)),
             dma((PLANES,)), dma((PLANES,)),
             dma((PLANES, 2)), dma((PLANES, 2)), dma((PLANES,)), dma((PLANES,)),
-            dma((4,)), dma((4,)), dma((2,)), dma((4,)),
+            dma((4,)), dma((4,)), dma((2,)), dma((4,)), dma((2,)),
             pltpu.VMEM((rows, dim), low), pltpu.VMEM((1, rows), full),
         ],
         compiler_params=pltpu.CompilerParams(

time: 58 us -> 58.2 us (level); the launches traced: 57.2 us -> 58 us
  Pallas kernels: 56.5 us -> 57.4 us
    pallas_call x1, Pallas kernels: 54.7 us -> 55.5 us  [per_device(): pl.pallas_call(kernel, out_shape=(jax.ShapeDtypeStruct((rows, dim), low),...]
where the time goes in v5:
time: 58.2 us; the launch traced here: 58 us
  Pallas kernels  57.4 us (99%)
  between operations  0.64 us (1%)
    pallas_call x1, Pallas kernels, per_device(): pl.pallas_call(kernel, out_shape=(jax.ShapeDtypeStruct((rows, dim), low),...  55.5 us
    pallas_call x1, Pallas kernels, per_device(): pl.pallas_call(copy_kernel, out_shape=tuple((jax.ShapeDtypeStruct(x.shape...  1.87 us

profile of v5, /device:TPU:16, one launch (start us, length us, event | category | flops | bytes accessed | tf_op | source)
XLA Modules:
  0.0 58.0 jit_solution(14094690547424351751)
XLA Ops:
  0.6 55.5 %shard_map.85 = (bf16[128,128]{1,0:T(8,128)(2,1)}, bf16[1024,128]{1,0:T(8,128)(2,1)}, bf16[1024,128]{1,0:T(8,128)(2,1)}) custom-call(bf16[128,128]{1,0:T(8,128)(2,1)} %bitcast.11, bf16[128,128]{1,0:T(8,128)(2,1)} %bitcast.12, bf16[128,128]{1,0:T(8,128)(2,1)} %bitcast.13, f32[1,128]{1,0:T(1,128)} %bitcast.14, bf16[8192,128]{1,0:T(8,128)(2,1)} %bitcast.9, ...), custom_call_target="tpu_custom_call" | custom-call | tf_op jit(solution)/shard_map/pallas_call | solution.py:356
  56.2 1.9 %shard_map.86 = (bf16[128,128]{1,0:T(8,128)(2,1)}, bf16[1024,128]{1,0:T(8,128)(2,1)}, bf16[1024,128]{1,0:T(8,128)(2,1)}) custom-call(bf16[128,128]{1,0:T(8,128)(2,1)} %get-tuple-element.9.refs_0_, bf16[1024,128]{1,0:T(8,128)(2,1)} %get-tuple-element.10.refs_1_, bf16[1024,128]{1,0:T(8,128)(2,1)} %get-tuple-element.11.refs_2_), custom_call_target="tpu_custom_call" | custom-call | tf_op jit(solution)/shard_map/pallas_call | solution.py:398

commit v6 on v4

--- a/solution.py
+++ b/solution.py
@@ -15,7 +15,7 @@
 PLANES = 8
 SPREAD = (4, 3, 6)
 ORDER = (2, 5, 0, 4, 7, 3, 1, 6)
-AHEAD = 5
+AHEAD = 7
 WINDOW = 8
 
 

time: 58 us -> 57.8 us (level); the launches traced: 57.2 us -> 57.6 us
  no operation moved by 1% of the time
where the time goes in v6:
time: 57.8 us; the launch traced here: 57.6 us
  Pallas kernels  57 us (99%)
  between operations  0.64 us (1%)
    pallas_call x1, Pallas kernels, per_device(): pl.pallas_call(kernel, out_shape=(jax.ShapeDtypeStruct((rows, dim), low),...  55.1 us
    pallas_call x1, Pallas kernels, per_device(): pl.pallas_call(copy_kernel, out_shape=tuple((jax.ShapeDtypeStruct(x.shape...  1.87 us

profile of v6, /device:TPU:16, one launch (start us, length us, event | category | flops | bytes accessed | tf_op | source)
XLA Modules:
  0.0 57.6 jit_solution(15386588679877075504)
XLA Ops:
  0.6 55.1 %shard_map.85 = (bf16[128,128]{1,0:T(8,128)(2,1)}, bf16[1024,128]{1,0:T(8,128)(2,1)}, bf16[1024,128]{1,0:T(8,128)(2,1)}) custom-call(bf16[128,128]{1,0:T(8,128)(2,1)} %bitcast.11, bf16[128,128]{1,0:T(8,128)(2,1)} %bitcast.12, bf16[128,128]{1,0:T(8,128)(2,1)} %bitcast.13, f32[1,128]{1,0:T(1,128)} %bitcast.14, bf16[8192,128]{1,0:T(8,128)(2,1)} %bitcast.9, ...), custom_call_target="tpu_custom_call" | custom-call | tf_op jit(solution)/shard_map/pallas_call | solution.py:339
  55.8 1.9 %shard_map.86 = (bf16[128,128]{1,0:T(8,128)(2,1)}, bf16[1024,128]{1,0:T(8,128)(2,1)}, bf16[1024,128]{1,0:T(8,128)(2,1)}) custom-call(bf16[128,128]{1,0:T(8,128)(2,1)} %get-tuple-element.9.refs_0_, bf16[1024,128]{1,0:T(8,128)(2,1)} %get-tuple-element.10.refs_1_, bf16[1024,128]{1,0:T(8,128)(2,1)} %get-tuple-element.11.refs_2_), custom_call_target="tpu_custom_call" | custom-call | tf_op jit(solution)/shard_map/pallas_call | solution.py:381
